TPU v7x, 128 devices: a whole 4x4x4 slice. The times are simulated.
128 devices in a mesh: cuts: 4 (over y), idx: 16 (over z_lo, x, core), br: 2 (over z_hi).
Axes of the slice: x: 4, y: 4, z: 4 (z_hi: 2, z_lo: 2; z = z_hi * 2 + z_lo), core: 2. Of those that a mesh axis runs over, the one named last changes fastest.
Arguments:
- stem_mantissa: bfloat16 [4, 2, 1024, 128, 512], P('cuts', None, 'idx', None, 'br'), may hold values from -6 to 6
- exponents: int32 [4, 1024, 128, 4], P('cuts', 'idx', None, 'br'), may hold values from -2 to 2
- branch: bfloat16 [2, 1024, 1024], P(None, None, 'br'), may hold values from -0.125 to 0.125
- closing: bfloat16 [2, 128, 512], P(None, 'idx', 'br'), may hold values from -0.00390625 to 0.00390625
- bitstrings: int32 [1024], replicated, may hold values from 0 to 1023
Outputs:
- new_stem: bfloat16 [4, 2, 1024, 128, 512], P('cuts', None, None, 'idx', 'br')
- amplitudes: float32 [2, 1024], replicated
All inputs are finite; a program needn't handle non-finite values.
Results may differ from a plain program's by a relative error of at most 0.0031.
Values may be sent and summed in bfloat16 or wider, within the bound.
A program may use at most 128 MiB of HBM per device.

v0:
```python
import jax
import jax.numpy as jnp
from jax import lax
from jax.sharding import PartitionSpec as P


def dequantize(mantissa, exponents):
    parts, k_local, r_count, q_local = mantissa.shape
    scale = jnp.exp2(exponents.astype(jnp.float32))
    shaped = (
        mantissa.astype(jnp.float32).reshape(parts, k_local, r_count, q_local // 128, 128)
        * scale[None, :, :, :, None]
    )
    return shaped.reshape(parts, k_local, r_count, q_local).astype(jnp.bfloat16)


def complex_matrix(block):
    real_part = block[0].T
    imag_part = block[1].T
    upper = jnp.concatenate([real_part, -imag_part], axis=1)
    lower = jnp.concatenate([imag_part, real_part], axis=1)
    return jnp.concatenate([upper, lower], axis=0)


def contract(branch, right_side):
    piece = lax.all_gather(branch, "br", axis=2, tiled=True)
    matrix = complex_matrix(piece)
    result = jnp.dot(matrix, right_side, preferred_element_type=jnp.float32)
    return result.reshape(2, piece.shape[2], right_side.shape[1])


def shards(stem_mantissa, exponents, branch, closing, bitstrings):
    values = dequantize(stem_mantissa[0], exponents[0])
    regrouped = lax.all_to_all(values, "idx", split_axis=2, concat_axis=1, tiled=True)
    k_all, r_local, q_local = regrouped.shape[1:]
    product = contract(branch, regrouped.reshape(2 * k_all, r_local * q_local))
    new_block = product.astype(jnp.bfloat16).reshape(2, product.shape[1], r_local, q_local)
    fields = new_block.astype(jnp.float32)
    env = closing.astype(jnp.float32)
    high = lax.Precision.HIGHEST
    real_part = jnp.einsum("lrq,rq->l", fields[0], env[0], precision=high) - jnp.einsum(
        "lrq,rq->l", fields[1], env[1], precision=high
    )
    imag_part = jnp.einsum("lrq,rq->l", fields[0], env[1], precision=high) + jnp.einsum(
        "lrq,rq->l", fields[1], env[0], precision=high
    )
    closed = jnp.stack([real_part, imag_part])
    open_count = fields.shape[1]
    selector = (bitstrings[:, None] == jnp.arange(open_count, dtype=jnp.int32)[None, :]).astype(
        jnp.float32
    )
    partial_amps = jnp.dot(closed, selector.T, precision=high)
    inner_sum = lax.psum(partial_amps, ("idx", "br"))
    total = lax.psum(inner_sum, "cuts")
    return (new_block[None], total)


def solution(mesh):
    return jax.shard_map(
        shards,
        mesh=mesh,
        in_specs=(
            P("cuts", None, "idx", None, "br"),
            P("cuts", "idx", None, "br"),
            P(None, None, "br"),
            P(None, "idx", "br"),
            P(),
        ),
        out_specs=(P("cuts", None, None, "idx", "br"), P()),
        check_vma=False,
    )
```

profile of v0, /device:TPU:1, one launch (start us, length us, event | category | flops | bytes accessed | tf_op | source)
XLA Modules:
  0.0 404.6 jit_solution(6859782162528874040)
XLA Ops:
  7.2 0.9 exponential_bitcast_fusion
  8.1 4.5 %copy.12 = f32[64,128,2]{2,0,1:T(8,128)} copy(f32[64,128,2]{1,2,0:T(2,128)S(1)} %exponential_bitcast_fusion) | data formatting | bytes 131072 | tf_op jit(solution)/shard_map/exp2 | solution.py:9
  12.5 11.8 %mul.13 = f32[64,128,2,128]{3,2,0,1:T(2,128)} broadcast(f32[64,128,2]{2,0,1:T(8,128)} %copy.12), dimensions={0,1,2} | broadcast | bytes 8454144 | tf_op jit(solution)/shard_map/mul | solution.py:11
  24.3 11.5 %mul.14 = f32[64,128,256]{2,0,1:T(8,128)} reshape(f32[64,128,2,128]{3,2,0,1:T(2,128)} %mul.13) | data formatting | bytes 16777216 | tf_op jit(solution)/shard_map/mul | solution.py:11
  35.8 11.8 %fusion = bf16[2,64,128,256]{3,1,0,2:T(8,128)(2,1)} fusion(bf16[1,2,64,128,256]{4,3,2,1,0:T(8,128)(2,1)} %param.5, f32[64,128,256]{2,0,1:T(8,128)} %mul.14), kind=kLoop, calls=%fused_computation.1 | loop fusion | flops 12582912 | bytes 25165824 | tf_op jit(solution)/shard_map/convert_element_type | solution.py:14
  47.6 7.3 %all-to-all-start = ((bf16[2,64,128,256]{3,1,0,2:T(8,128)(2,1)}), bf16[2,64,128,256]{3,1,0,2:T(8,128)(2,1)}, u32[]{:S(2)}, u32[]{:S(2)}) async-start(bf16[2,64,128,256]{3,1,0,2:T(8,128)(2,1)} %fusion), calls=%async_computation | async-start | bytes 16777216 | tf_op jit(solution)/shard_map/all_to_all | solution.py:34
  54.9 0.2 all-gather.2.cloned.1.call-start
  55.1 0.5 all-gather.2.cloned.1.call-update
  55.7 0.0 copy-done.1
  55.7 139.0 %all-gather.2.cloned.1.call-done = bf16[2,1024,1024]{2,1,0:T(8,128)(2,1)} async-done(((bf16[2,1024,512]{2,1,0:T(8,128)(2,1)}), bf16[2,1024,1024]{2,1,0:T(8,128)(2,1)}) %all-gather.2.cloned.1.call-update) | async-done | bytes 4194320 | tf_op jit(solution)/shard_map/all_gather | solution.py:26
  194.7 1.7 fusion.19
  196.4 2.7 slice_bitcast_fusion
  199.1 36.6 %maximum_maximum_fusion = bf16[2048,2048]{0,1:T(8,128)(2,1)} fusion(bf16[1024,1024]{0,1:T(8,128)(2,1)S(1)} %get-tuple-element.5, bf16[1024,1024]{0,1:T(8,128)(2,1)S(1)} %get-tuple-element.4, bf16[1024,1024]{0,1:T(8,128)(2,1)S(1)} %fusion.19), kind=kLoop, calls=%fused_computation.2 | loop fusion | flops 33554432 | bytes 14680064 | tf_op jit(solution)/shard_map/concatenate | solution.py:22
  235.7 12.5 %copy.10 = bf16[2048,2048]{1,0:T(8,128)(2,1)} copy(bf16[2048,2048]{0,1:T(8,128)(2,1)} %maximum_maximum_fusion) | data formatting | bytes 16777216 | tf_op jit(solution)/shard_map/concatenate | solution.py:22
  248.2 0.0 all-to-all-done
  248.2 15.4 %copy.39 = bf16[2,64,16,8,256]{4,3,1,2,0:T(8,128)(2,1)} copy(bf16[2,64,16,8,256]{4,1,0,3,2:T(8,128)(2,1)} %bitcast.9) | data formatting | bytes 16777216 | tf_op jit(solution)/shard_map/all_to_all | solution.py:34
  263.6 13.5 %reshape.36 = bf16[2048,2048,1]{1,0,2:T(8,128)(2,1)} reshape(bf16[2,16,64,8,256]{4,3,2,1,0:T(8,128)(2,1)} %bitcast.49) | data formatting | bytes 16777216 | tf_op jit(solution)/shard_map/reshape | solution.py:36
  277.1 22.2 %convolution_convert_fusion = bf16[2,1024,2048]{2,1,0:T(8,128)(2,1)S(1)} fusion(bf16[2,1024,2048]{2,1,0:T(8,128)(2,1)} %bitcast.52, bf16[2048,2048,1]{1,0,2:T(8,128)(2,1)} %reshape.36), kind=kOutput, calls=%fused_computation.4 | convolution fusion | flops 17184063488 | bytes 25165824 | tf_op jit(solution)/shard_map/dot_general | solution.py:28
  299.3 0.0 copy-start
  299.3 1.6 fusion.20
  300.9 1.8 copy-done
  302.7 1.5 copy.19
  304.2 1.5 copy.20
  305.7 1.2 fusion.8
  306.9 1.2 fusion.6
  308.1 1.2 fusion.4
  309.3 1.2 fusion.2
  310.5 0.0 copy-done.2
  310.5 2.0 fusion.1
  312.5 65.0 %psum.14 = f32[2,1024]{1,0:T(2,128)S(1)} all-reduce(f32[2,1024]{1,0:T(2,128)S(1)} %fusion.1), channel_id=1, replica_groups=mesh['cuts'=4,'idx'=16,'br'=2] {'idx','br'}, use_global_device_ids=true, to_apply=%region_0.0 | all-reduce | flops 2048 | bytes 16384 | tf_op jit(solution)/shard_map/psum | solution.py:53
  377.6 9.6 %psum.15 = f32[2,1024]{1,0:T(2,128)} all-reduce(f32[2,1024]{1,0:T(2,128)S(1)} %psum.14), channel_id=1, replica_groups=mesh['cuts'=4,'idx'=16,'br'=2] {'cuts'}, use_global_device_ids=true, to_apply=%region_1.0 | all-reduce | flops 2048 | bytes 16384 | tf_op jit(solution)/shard_map/psum | solution.py:54
  387.1 10.5 %copy.18 = bf16[256,8,8,256]{3,2,1,0:T(8,128)(2,1)} copy(bf16[256,8,8,256]{3,1,2,0:T(8,128)(2,1)} %bitcast.48) | data formatting | bytes 16777216
  (5 shorter events, 0.0 us)
Async XLA Ops:
  47.6 8.0 %copy-start.1 = (bf16[2,8,256]{2,1,0:T(8,128)(2,1)S(1)}, bf16[2,8,256]{2,1,0:T(8,128)(2,1)}, u32[]{:S(2)}) copy-start(bf16[2,8,256]{2,1,0:T(8,128)(2,1)} %param.8) | copy-start | bytes 24580
  47.6 200.6 %all-to-all-start = ((bf16[2,64,128,256]{3,1,0,2:T(8,128)(2,1)}), bf16[2,64,128,256]{3,1,0,2:T(8,128)(2,1)}, u32[]{:S(2)}, u32[]{:S(2)}) async-start(bf16[2,64,128,256]{3,1,0,2:T(8,128)(2,1)} %fusion), calls=%async_computation | async-start | bytes 16777216 | tf_op jit(solution)/shard_map/all_to_all | solution.py:34
  54.9 139.8 %all-gather.2.cloned.1.call-start = ((), (), s32[]{:S(2)}) async-start(), calls=%async_computation.1 | async-start | bytes 6291456 | tf_op jit(solution)/shard_map/all_gather | solution.py:26
  299.3 3.4 copy-start
  308.1 2.4 copy-start.2
Sparse Core Ops, SparseCore 0:
  57.4 137.2 all-gather.1
where the time goes:
time: 412 us; the launch traced here: 405 us
  waiting for transfers between devices  140 us (34%)
  local copies, waits for them, and re-layouts  88.6 us (22%)
  blocking collectives  74.6 us (18%)
  other arithmetic  51.1 us (12%)
  matrix products  29 us (7%)
  between operations  14.3 us (3%)
  starting transfers between devices  7.51 us (2%)
    all_gather x1, waiting for transfers between devices, contract(): piece = lax.all_gather(branch, 'br', axis=2, tiled=True)  139 us
    psum x1, blocking collectives, shards(): inner_sum = lax.psum(partial_amps, ('idx', 'br'))  65 us
    concatenate x1, other arithmetic, complex_matrix(): return jnp.concatenate([upper, lower], axis=0)  36.6 us
    mul x2, local copies, waits for them, and re-layouts, dequantize(): mantissa.astype(jnp.float32)  23.3 us
    dot_general x1, matrix products, contract(): result = jnp.dot(matrix, right_side, preferred_element_type=jnp.float32)  22.2 us
    all_to_all x1, local copies, waits for them, and re-layouts, shards(): lax.all_to_all(values, 'idx', split_axis=2, concat_axis=1, tiled=True)  15.4 us
    unnamed x9, local copies, waits for them, and re-layouts  15.2 us
    reshape x1, local copies, waits for them, and re-layouts, shards(): product = contract(branch, regrouped.reshape(2 * k_all, r_local * q_local))  13.5 us
  transfers between devices with their start and end apart: 2, of which 1 were waited for; matrix products, arithmetic and copies ran while one was open for 13% of the time, Pallas kernels for 0%

commit v1 on v0

v1 whole, which is shorter than its diff:
```python
import jax
import jax.numpy as jnp
from jax import lax
from jax.experimental import pallas as pl
from jax.experimental.pallas import tpu as pltpu
from jax.sharding import PartitionSpec as P

MESH = pl.DeviceIdType.MESH
F32 = jnp.float32
BF16 = jnp.bfloat16
ROUNDS = 8
AHEAD = 3


def full_wait(ref, sem):
    pltpu.make_async_copy(ref, ref, sem).wait()


def contract_kernel(
    stem, expo, branch, closing, bits,
    product, amps,
    inbuf, raw_exp, scale, tiles, sendbuf, recvbuf, own_half, other_half, matrix,
    env_raw, env, bits_v, part, part_in, mid, mid_in, total_in, amps_v,
    in_sem, small_sem, half_sem, send_sem, recv_sem, half_send, half_recv, fwd_send, fwd_recv,
    env_send, env_recv, part_send, part_recv, mid_send, mid_recv, total_send, total_recv, amp_sem,
):
    c = lax.axis_index("cuts")
    me = lax.axis_index("idx")
    b = lax.axis_index("br")
    core = me % 2
    x = (me // 2) % 4
    z = me // 8
    k_local = sendbuf.shape[4]

    def group(n):
        dz = 1 - (n // 2) % 2
        dx = (2 + n % 2) * (1 - n // 4) + (1 - n % 2) * (n // 4)
        return ((z + dz) % 2) * 4 + (x + dx) % 4

    def peer(step):
        return (c, (me + step) % 16, b)

    def outer(step):
        spot = (c * 2 + b + step) % 8
        return (spot // 2, me, spot % 2)

    twin = (c, (me + 8) % 16, 1 - b)
    sibling = (c, me + 1 - 2 * core, b)

    def load(n, slot):
        return pltpu.make_async_copy(
            stem.at[:, :, pl.ds(pl.multiple_of(group(n) * 16, 16), 16), :], inbuf.at[slot], in_sem.at[slot]
        )

    exp_copy = pltpu.make_async_copy(expo, raw_exp, small_sem.at[0])
    exp_copy.start()
    load(0, 0).start()
    load(1, 1).start()

    barrier = pltpu.get_barrier_semaphore()
    for step in range(1, 16):
        pl.semaphore_signal(barrier, inc=1, device_id=peer(step), device_id_type=MESH)
    for step in range(1, 8):
        pl.semaphore_signal(barrier, inc=1, device_id=outer(step), device_id_type=MESH)
    pl.semaphore_signal(barrier, inc=1, device_id=twin, device_id_type=MESH)

    bits_copy = pltpu.make_async_copy(bits, bits_v, small_sem.at[1])
    bits_copy.start()
    own_copy = pltpu.make_async_copy(branch, own_half, half_sem)
    own_copy.start()

    exp_copy.wait()
    for h in range(2):
        shifted = raw_exp[:, h, :] + 2
        low = (1 + shifted % 2).astype(F32)
        middle = (1 + 3 * ((shifted // 2) % 2)).astype(F32)
        high = (1 + 15 * ((shifted // 4) % 2)).astype(F32)
        scale[h] = 0.25 * low * middle * high

    def message(n, dc, j):
        cc = (core + dc) % 2
        return pltpu.make_async_remote_copy(
            src_ref=sendbuf.at[n, cc, j],
            dst_ref=recvbuf.at[j, :, pl.ds(pl.multiple_of(me * k_local, k_local), k_local), :],
            send_sem=send_sem.at[j],
            recv_sem=recv_sem.at[j],
            device_id=(c, group(n) * 2 + cc, b),
            device_id_type=MESH,
        )

    def keep(j):
        return pltpu.make_async_copy(
            sendbuf.at[7, core, j],
            recvbuf.at[j, :, pl.ds(pl.multiple_of(me * k_local, k_local), k_local), :],
            recv_sem.at[j],
        )

    def regroup(n, slot):
        g = group(n)
        turn = (128 - g * 16) % 128
        load(n, slot).wait()

        def step(kb, carry):
            k0 = pl.multiple_of(kb * 16, 16)
            factors = [pltpu.roll(scale[h, pl.ds(k0, 16), :], turn, 1) for h in range(2)]
            for p in range(2):
                for h in range(2):
                    block = inbuf[slot, p, pl.ds(k0, 16), :, h * 128:(h + 1) * 128]
                    tiles[p, h] = block.astype(F32).reshape(256, 128)
            for h in range(2):
                for r in range(16):
                    factor = jnp.broadcast_to(factors[h][:, r:r + 1], (16, 128))
                    for p in range(2):
                        rows = tiles[p, h, pl.ds(r, 16, stride=16), :] * factor
                        sendbuf[n, r // 8, r % 8, p, pl.ds(k0, 16), h * 128:(h + 1) * 128] = rows.astype(BF16)
            return carry

        lax.fori_loop(0, k_local // 16, step, 0)

    regroup(0, 0)
    load(2, 0).start()
    pl.semaphore_wait(barrier, 23)

    def env_copy(step):
        return pltpu.make_async_remote_copy(
            src_ref=closing, dst_ref=env_raw.at[me], send_sem=env_send, recv_sem=env_recv,
            device_id=peer(step), device_id_type=MESH,
        )

    half_rows = own_half.shape[1] // 2
    quarter = half_rows // 4

    def half_copy(t):
        rows = pl.ds(pl.multiple_of(core * half_rows + t * quarter, quarter), quarter)
        return pltpu.make_async_remote_copy(
            src_ref=branch.at[:, rows, :], dst_ref=other_half.at[:, rows, :],
            send_sem=half_send, recv_sem=half_recv, device_id=twin, device_id_type=MESH,
        )

    mine = pl.ds(pl.multiple_of(core * half_rows, half_rows), half_rows)
    theirs = pl.ds(pl.multiple_of((1 - core) * half_rows, half_rows), half_rows)
    forward = pltpu.make_async_remote_copy(
        src_ref=other_half.at[:, mine, :], dst_ref=other_half.at[:, mine, :],
        send_sem=fwd_send, recv_sem=fwd_recv, device_id=sibling, device_id_type=MESH,
    )

    message(0, 0, 0).start()
    message(0, 1, 0).start()
    for t in range(4):
        half_copy(t).start()
    for step in range(1, 16):
        env_copy(step).start()
    pltpu.make_async_copy(closing, env_raw.at[me], env_recv).start()

    def produce(n, carry):
        slot = n % 2
        regroup(n, slot)

        @pl.when(n < 6)
        def _():
            load(n + 2, slot).start()

        message(n, 0, 0).start()
        message(n, 1, 0).start()
        return carry

    lax.fori_loop(1, 7, produce, 0)
    regroup(7, 1)
    keep(0).start()
    message(7, 1, 0).start()

    def send_round(j):
        def one(dc):
            def start(n, carry):
                message(n, dc, j).start()
                return carry

            return start

        lax.fori_loop(0, 7, one(0), 0)
        keep(j).start()
        message(7, 1, j).start()
        lax.fori_loop(0, 7, one(1), 0)

    for j in range(1, AHEAD):
        send_round(j)

    k_all = own_half.shape[1]
    l_half = own_half.shape[2]

    def fill(half, where):
        def step(kb, carry):
            k0 = pl.multiple_of(kb * 128, 128)
            row = pl.multiple_of(where * l_half, l_half)
            real = half[0, pl.ds(k0, 128), :].T
            imag = half[1, pl.ds(k0, 128), :].T
            matrix[pl.ds(row, l_half), pl.ds(k0, 128)] = real
            matrix[pl.ds(row, l_half), pl.ds(k_all + k0, 128)] = -imag
            matrix[pl.ds(2 * l_half + row, l_half), pl.ds(k0, 128)] = imag
            matrix[pl.ds(2 * l_half + row, l_half), pl.ds(k_all + k0, 128)] = real
            return carry

        lax.fori_loop(0, k_all // 128, step, 0)

    own_copy.wait()
    fill(own_half, b)

    full_wait(env_raw, env_recv)
    env[...] = env_raw[...].astype(F32)

    def gather_env(n, sums):
        g = group(n)

        def row(t, sums):
            cc = t // 8
            j = t % 8
            new = []
            for p in range(2):
                values = sendbuf[n, cc, j, p].astype(F32)
                for e in range(2):
                    weighted = values * env[2 * g + cc, e, pl.ds(j, 1), :]
                    new.append(sums[2 * p + e] + (weighted[:, :128] + weighted[:, 128:]))
            return tuple(new)

        return lax.fori_loop(0, 16, row, sums)

    zero = jnp.zeros((k_local, 128), F32)
    sums = lax.fori_loop(0, 8, gather_env, (zero,) * 4)
    w = [jnp.sum(s, axis=1, keepdims=True) for s in sums]
    w_real = w[0] - w[3]
    w_imag = w[1] + w[2]

    full_wait(other_half.at[:, mine, :], half_recv)
    forward.start()
    full_wait(other_half.at[:, theirs, :], fwd_recv)
    fill(other_half, 1 - b)

    k_mine = pl.ds(pl.multiple_of(me * k_local, k_local), k_local)
    blocks = l_half // 128
    for half, where in ((own_half, b), (other_half, 1 - b)):
        real = half[0, k_mine, :].astype(F32)
        imag = half[1, k_mine, :].astype(F32)
        closed_real = jnp.sum(real * w_real - imag * w_imag, axis=0, keepdims=True)
        closed_imag = jnp.sum(real * w_imag + imag * w_real, axis=0, keepdims=True)
        for t in range(blocks):
            part[where * blocks + t] = closed_real[:, t * 128:(t + 1) * 128]
            part[2 * blocks + where * blocks + t] = closed_imag[:, t * 128:(t + 1) * 128]

    def part_copy(step):
        to = (me + step) % 16
        return pltpu.make_async_remote_copy(
            src_ref=part.at[to], dst_ref=part_in.at[me], send_sem=part_send, recv_sem=part_recv,
            device_id=(c, to, b), device_id_type=MESH,
        )

    def mid_copy(step):
        return pltpu.make_async_remote_copy(
            src_ref=mid.at[0], dst_ref=mid_in.at[c * 2 + b], send_sem=mid_send, recv_sem=mid_recv,
            device_id=outer(step), device_id_type=MESH,
        )

    def total_copy(step):
        return pltpu.make_async_remote_copy(
            src_ref=mid.at[1], dst_ref=total_in.at[me], send_sem=total_send, recv_sem=total_recv,
            device_id=peer(step), device_id_type=MESH,
        )

    for step in range(1, 16):
        part_copy(step).start()
    pltpu.make_async_copy(part.at[me], part_in.at[me], part_recv).start()

    def reduce_stage(j):
        @pl.when(j == 2)
        def _():
            full_wait(part_in, part_recv)
            mid[0] = jnp.sum(part_in[...], axis=0)
            for step in range(1, 8):
                mid_copy(step).start()
            pltpu.make_async_copy(mid.at[0], mid_in.at[c * 2 + b], mid_recv).start()

        @pl.when(j == 4)
        def _():
            full_wait(mid_in, mid_recv)
            mid[1] = jnp.sum(mid_in[...], axis=0)
            for step in range(1, 16):
                total_copy(step).start()
            pltpu.make_async_copy(mid.at[1], total_in.at[me], total_recv).start()

        @pl.when(j == 6)
        def _():
            full_wait(total_in, total_recv)
            bits_copy.wait()
            chosen = bits_v[...]
            found = jnp.zeros((8, chosen.shape[1]), F32)
            for t in range(2 * blocks):
                rows = [total_in[t], total_in[2 * blocks + t], jnp.zeros((6, 128), F32)]
                spots = lax.broadcasted_iota(jnp.int32, (128, chosen.shape[1]), 0) + t * 128
                pick = jnp.where(spots == chosen, 1.0, 0.0).astype(F32)
                found = found + jnp.dot(
                    jnp.concatenate(rows, axis=0), pick, precision=lax.Precision.HIGHEST, preferred_element_type=F32
                )
            amps_v[...] = found[:2]
            pltpu.make_async_copy(amps_v, amps, amp_sem).start()

    m_block = 512

    def chunk(j, carry):
        @pl.when(j + AHEAD < ROUNDS)
        def _():
            send_round(j + AHEAD)

        full_wait(recvbuf.at[j], recv_sem.at[j])

        def rows(m, carry):
            m0 = pl.multiple_of(m * m_block, m_block)
            right = recvbuf[j].reshape(2 * k_all, recvbuf.shape[3])
            result = jnp.dot(matrix[pl.ds(m0, m_block), :], right, preferred_element_type=F32)
            for h in range(2):
                product[h, pl.ds(m0 * ROUNDS + j, m_block, stride=ROUNDS), :] = result[:, h * 128:(h + 1) * 128]
            return carry

        lax.fori_loop(0, matrix.shape[0] // m_block, rows, 0)
        reduce_stage(j)
        return carry

    lax.fori_loop(0, ROUNDS, chunk, 0)

    for j in range(ROUNDS):
        full_wait(recvbuf.at[j, :, pl.ds(0, 15 * k_local), :], send_sem.at[j])
    full_wait(other_half.at[:, mine, :], half_send)
    full_wait(other_half.at[:, mine, :], fwd_send)
    full_wait(env_raw.at[pl.ds(0, 15)], env_send)
    full_wait(part_in.at[pl.ds(0, 15)], part_send)
    full_wait(mid_in.at[pl.ds(0, 7)], mid_send)
    full_wait(total_in.at[pl.ds(0, 15)], total_send)
    full_wait(amps_v, amp_sem)


def write_kernel(product, amps_in, out, amps, staging, out_sem):
    blocks, rows = staging.shape[:2]
    per_part = out.shape[1] // rows

    def copy(t):
        return pltpu.make_async_copy(
            staging.at[t], out.at[t // per_part, pl.ds((t % per_part) * rows, rows)], out_sem.at[t]
        )

    def step(t, carry):
        for h in range(2):
            block = product[h, pl.ds(pl.multiple_of(t * rows * 8, rows * 8), rows * 8), :]
            staging[t, :, :, h * 128:(h + 1) * 128] = block.reshape(rows, 8, 128).astype(BF16)
        copy(t).start()
        return carry

    lax.fori_loop(0, blocks, step, 0)
    amps[...] = amps_in[...]

    def finish(t, carry):
        copy(t).wait()
        return carry

    lax.fori_loop(0, blocks, finish, 0)


def shards(stem_mantissa, exponents, branch, closing, bitstrings):
    stem = stem_mantissa[0]
    k_local, r_all, q_local = stem.shape[1:]
    k_all, l_half = branch.shape[1:]
    l_all = 2 * l_half
    r_local = closing.shape[1]
    expo = jnp.transpose(exponents[0], (0, 2, 1))
    bits = bitstrings.reshape(1, -1)
    dma = pltpu.SemaphoreType.DMA
    hbm = pl.BlockSpec(memory_space=pl.ANY)
    vmem = pl.BlockSpec(memory_space=pltpu.VMEM)
    product, amps = pl.pallas_call(
        contract_kernel,
        out_shape=(
            pltpu.VMEM((2, 2 * l_all * r_local, 128), F32),
            jax.ShapeDtypeStruct((2, bits.shape[1]), F32),
        ),
        in_specs=[hbm] * 5,
        out_specs=(vmem, hbm),
        scratch_shapes=[
            pltpu.VMEM((2, 2, k_local, 16, q_local), BF16),
            pltpu.VMEM(expo.shape, jnp.int32),
            pltpu.VMEM((2, k_local, r_all), F32),
            pltpu.VMEM((2, 2, 256, 128), F32),
            pltpu.VMEM((8, 2, r_local, 2, k_local, q_local), BF16),
            pltpu.VMEM((r_local, 2, k_all, q_local), BF16),
            pltpu.VMEM((2, k_all, l_half), BF16),
            pltpu.VMEM((2, k_all, l_half), BF16),
            pltpu.VMEM((2 * l_all, 2 * k_all), BF16),
            pltpu.VMEM((16,) + closing.shape, BF16),
            pltpu.VMEM((16,) + closing.shape, F32),
            pltpu.VMEM(bits.shape, jnp.int32),
            pltpu.VMEM((16, 1, 128), F32),
            pltpu.VMEM((16, 1, 128), F32),
            pltpu.VMEM((2, 1, 128), F32),
            pltpu.VMEM((8, 1, 128), F32),
            pltpu.VMEM((16, 1, 128), F32),
            pltpu.VMEM((2, bits.shape[1]), F32),
            dma((2,)), dma((2,)), dma,
            dma((ROUNDS,)), dma((ROUNDS,)),
            dma, dma, dma, dma, dma, dma, dma, dma, dma, dma, dma, dma, dma,
        ],
        compiler_params=pltpu.CompilerParams(
            collective_id=0, has_side_effects=True, vmem_limit_bytes=44 * 2**20
        ),
        cost_estimate=pl.CostEstimate(
            flops=2 * (2 * k_all) * (2 * l_all) * r_local * q_local, bytes_accessed=2 * stem.size, transcendentals=0
        ),
        name="exchange_and_contract",
    )(stem, expo, branch, closing, bits)

    rows = 128
    new_block, amps = pl.pallas_call(
        write_kernel,
        out_shape=(
            jax.ShapeDtypeStruct((2, l_all, r_local, q_local), BF16),
            jax.ShapeDtypeStruct(amps.shape, F32),
        ),
        in_specs=[vmem, vmem],
        out_specs=(hbm, vmem),
        scratch_shapes=[
            pltpu.VMEM((2 * l_all // rows, rows, r_local, q_local), BF16),
            dma((2 * l_all // rows,)),
        ],
        compiler_params=pltpu.CompilerParams(vmem_limit_bytes=40 * 2**20),
        name="round_and_write",
    )(pltpu.with_memory_space_constraint(product, pltpu.VMEM), amps)
    return (new_block[None], amps)


def solution(mesh):
    return jax.shard_map(
        shards,
        mesh=mesh,
        in_specs=(
            P("cuts", None, "idx", None, "br"),
            P("cuts", "idx", None, "br"),
            P(None, None, "br"),
            P(None, "idx", "br"),
            P(),
        ),
        out_specs=(P("cuts", None, None, "idx", "br"), P()),
        check_vma=False,
    )
```

time: 412 us -> 114 us (0.28); the launches traced: 405 us -> 114 us
  waiting for transfers between devices: 140 us -> 0 us
  Pallas kernels: 0 us -> 113 us
  local copies, waits for them, and re-layouts: 88.6 us -> 0 us
  blocking collectives: 74.6 us -> 0 us
  other arithmetic: 51.1 us -> 0 us
  matrix products: 29 us -> 0 us
  between operations: 14.3 us -> 0.64 us
  starting transfers between devices: 7.51 us -> 0 us
    all_gather x1 -> x0, waiting for transfers between devices: 139 us -> none  [contract(): piece = lax.all_gather(branch, 'br', axis=2, tiled=True)]
    pallas_call x0 -> x2, Pallas kernels: none -> 113 us  [the longest x1 109 us: shards(): pl.pallas_call(contract_kernel, out_shape=(pltpu.VMEM((2, 2 * l_all * r_l...]
    psum x2 -> x0, blocking collectives: 74.6 us -> none  [the longest x1 65 us: shards(): inner_sum = lax.psum(partial_amps, ('idx', 'br'))]
    concatenate x1 -> x0, other arithmetic: 36.6 us -> none  [complex_matrix(): return jnp.concatenate([upper, lower], axis=0)]
    dot_general x6 -> x0, matrix products: 29 us -> none  [the longest x1 22.2 us: contract(): result = jnp.dot(matrix, right_side, preferred_element_type=jnp.float32)]
    mul x2 -> x0, local copies, waits for them, and re-layouts: 23.3 us -> none  [dequantize(): mantissa.astype(jnp.float32)]
    all_to_all x1 -> x0, local copies, waits for them, and re-layouts: 15.4 us -> none  [shards(): lax.all_to_all(values, 'idx', split_axis=2, concat_axis=1, tiled=True)]
    unnamed x9 -> x0, local copies, waits for them, and re-layouts: 15.2 us -> none
  transfers between devices with their start and end apart: 2 -> 0, of which waited for: 1 -> 0; matrix products, arithmetic and copies ran while one was open for 13% -> 0% of each run, Pallas kernels for 0% -> 0%
where the time goes in v1:
time: 114 us
  Pallas kernels  113 us (99%)
    pallas_call x1, Pallas kernels, shards(): pl.pallas_call(contract_kernel, out_shape=(pltpu.VMEM((2, 2 * l_all * r_l...  109 us
    pallas_call x1, Pallas kernels, shards(): pl.pallas_call(write_kernel, out_shape=(jax.ShapeDtypeStruct((2, l_all, r...  4.78 us

profile of v1, /device:TPU:1, one launch (start us, length us, event | category | flops | bytes accessed | tf_op | source)
XLA Modules:
  0.0 114.1 jit_solution(2421428574434386271)
XLA Ops:
  0.6 108.7 %exchange_and_contract.1 = (f32[2,16384,128]{2,1,0:T(8,128)S(1)}, f32[2,1024]{1,0:T(2,128)}) custom-call(bf16[2,64,128,256]{3,2,1,0:T(8,128)(2,1)} %bitcast.6, s32[64,2,128]{2,1,0:T(2,128)} %bitcast.8, bf16[2,1024,512]{2,1,0:T(8,128)(2,1)} %branch.1, bf16[2,8,256]{2,1,0:T(8,128)(2,1)} %closing.1, s32[1,1024]{1,0:T(1,128)} %bitcast.9), custom_call_target="tpu_custom_call" | custom-call | flops 17179869184 | bytes 8388608 | tf_op jit(solution)/shard_map/exchange_and_contract/pallas_call | solution.py:376
  109.3 4.8 %round_and_write.1 = (bf16[2,1024,8,256]{3,2,1,0:T(8,128)(2,1)}, f32[2,1024]{1,0:T(2,128)}) custom-call(f32[2,16384,128]{2,1,0:T(8,128)S(1)} %get-tuple-element.6.product, f32[2,1024]{1,0:T(2,128)} %get-tuple-element.7.amps_in), custom_call_target="tpu_custom_call" | custom-call | tf_op jit(solution)/shard_map/round_and_write/pallas_call | solution.py:417

commit v2 on v1

v2 whole, which is shorter than its diff:
```python
import jax
import jax.numpy as jnp
from jax import lax
from jax.experimental import pallas as pl
from jax.experimental.pallas import tpu as pltpu
from jax.sharding import PartitionSpec as P

MESH = pl.DeviceIdType.MESH
F32 = jnp.float32
BF16 = jnp.bfloat16
ROUNDS = 8
DEPTH = 2


def full_wait(ref, sem):
    pltpu.make_async_copy(ref, ref, sem).wait()


def contract_kernel(
    stem, expo, branch, closing, bits,
    product, latest, matrix, amps,
    inbuf, raw_exp, scale, tiles, sendbuf, recvbuf, own_half, other_half, other_rows,
    env_raw, env, bits_v, part, part_in, mid, mid_in, total_in, amps_v,
    in_sem, small_sem, half_sem, send_sem, recv_sem, near_send, half_send, half_recv, fwd_send, fwd_recv,
    rows_send, rows_recv, env_send, env_recv, share_send, share_recv, part_send, part_recv, mid_send, mid_recv, total_send, total_recv, amp_sem,
    ready, twin_ready,
):
    c = lax.axis_index("cuts")
    me = lax.axis_index("idx")
    b = lax.axis_index("br")
    core = me % 2
    x = (me // 2) % 4
    z = me // 8
    k_local, q_local = sendbuf.shape[4:]

    def group(n):
        dz = 1 - (n // 2) % 2
        dx = (2 + n % 2) * (1 - n // 4) + (1 - n % 2) * (n // 4)
        return ((z + dz) % 2) * 4 + (x + dx) % 4

    def peer(step):
        return (c, (me + step) % 16, b)

    rank = b * 4 + c

    def outer(q):
        return (q % 4, me, q // 4)

    twin = (c, (me + 8) % 16, 1 - b)
    sibling = (c, me + 1 - 2 * core, b)

    def load(n, slot):
        return pltpu.make_async_copy(
            stem.at[:, :, pl.ds(pl.multiple_of(group(n) * 16, 16), 16), :], inbuf.at[slot], in_sem.at[slot]
        )

    exp_copy = pltpu.make_async_copy(expo, raw_exp, small_sem.at[0])
    exp_copy.start()
    load(0, 0).start()
    load(1, 1).start()

    barrier = pltpu.get_barrier_semaphore()
    for step in range(1, 16):
        pl.semaphore_signal(barrier, inc=1, device_id=peer(step), device_id_type=MESH)

    @pl.when(b == 0)
    def _():
        pl.semaphore_signal(barrier, inc=1, device_id=twin, device_id_type=MESH)

    for q in range(1, 8):
        @pl.when(q > rank)
        def _(q=q):
            pl.semaphore_signal(barrier, inc=1, device_id=outer(q), device_id_type=MESH)

    bits_copy = pltpu.make_async_copy(bits, bits_v, small_sem.at[1])
    bits_copy.start()
    own_copy = pltpu.make_async_copy(branch, own_half, half_sem)
    own_copy.start()

    exp_copy.wait()
    for h in range(2):
        shifted = raw_exp[:, h, :] + 2
        low = (1 + shifted % 2).astype(F32)
        middle = (1 + 3 * ((shifted // 2) % 2)).astype(F32)
        high = (1 + 15 * ((shifted // 4) % 2)).astype(F32)
        scale[h] = 0.25 * low * middle * high

    def landing(dc, j, final):
        rows = pl.ds(pl.multiple_of((me // 2) * k_local, k_local), k_local)
        return latest.at[dc, :, rows, :] if final else recvbuf.at[j, dc, :, rows, :]

    def message(n, dc, j, sem, final=False):
        cc = (core + dc) % 2
        return pltpu.make_async_remote_copy(
            src_ref=sendbuf.at[n, cc, j],
            dst_ref=landing(dc, j, final),
            send_sem=sem,
            recv_sem=recv_sem.at[2 * j + dc],
            device_id=(c, group(n) * 2 + cc, b),
            device_id_type=MESH,
        )

    def keep(j, final=False):
        return pltpu.make_async_copy(sendbuf.at[7, core, j], landing(0, j, final), recv_sem.at[2 * j])

    def regroup(n, slot):
        g = group(n)
        turn = (128 - g * 16) % 128
        load(n, slot).wait()

        def step(kb, carry):
            k0 = pl.multiple_of(kb * 16, 16)
            factors = [pltpu.roll(scale[h, pl.ds(k0, 16), :], turn, 1) for h in range(2)]
            for p in range(2):
                for h in range(2):
                    block = inbuf[slot, p, pl.ds(k0, 16), :, h * 128:(h + 1) * 128]
                    tiles[p, h] = block.astype(F32).reshape(256, 128)
            for h in range(2):
                for r in range(16):
                    factor = jnp.broadcast_to(factors[h][:, r:r + 1], (16, 128))
                    for p in range(2):
                        rows = tiles[p, h, pl.ds(r, 16, stride=16), :] * factor
                        sendbuf[n, r // 8, r % 8, p, pl.ds(k0, 16), h * 128:(h + 1) * 128] = rows.astype(BF16)
            return carry

        lax.fori_loop(0, k_local // 16, step, 0)

    pl.semaphore_wait(barrier, 15 + rank + b)

    chip = me // 2

    def env_copy(step):
        return pltpu.make_async_remote_copy(
            src_ref=closing, dst_ref=env_raw.at[core, chip], send_sem=env_send, recv_sem=env_recv,
            device_id=peer(2 * step), device_id_type=MESH,
        )

    env_share = pltpu.make_async_remote_copy(
        src_ref=env_raw.at[core], dst_ref=env_raw.at[core], send_sem=share_send, recv_sem=share_recv,
        device_id=sibling, device_id_type=MESH,
    )

    half_rows = own_half.shape[1] // 2
    quarter = half_rows // 4

    def half_copy(t):
        rows = pl.ds(pl.multiple_of(core * half_rows + t * quarter, quarter), quarter)
        return pltpu.make_async_remote_copy(
            src_ref=branch.at[:, rows, :], dst_ref=other_half.at[:, rows, :],
            send_sem=half_send, recv_sem=half_recv, device_id=twin, device_id_type=MESH,
        )

    mine = pl.ds(pl.multiple_of(core * half_rows, half_rows), half_rows)
    theirs = pl.ds(pl.multiple_of((1 - core) * half_rows, half_rows), half_rows)
    forward = pltpu.make_async_remote_copy(
        src_ref=other_half.at[:, mine, :], dst_ref=other_half.at[:, mine, :],
        send_sem=fwd_send, recv_sem=fwd_recv, device_id=sibling, device_id_type=MESH,
    )
    twin_rows = pltpu.make_async_remote_copy(
        src_ref=branch.at[:, pl.ds(pl.multiple_of(((me + 8) % 16) * k_local, k_local), k_local), :],
        dst_ref=other_rows, send_sem=rows_send, recv_sem=rows_recv, device_id=twin, device_id_type=MESH,
    )

    for step in range(1, 8):
        env_copy(step).start()
    pltpu.make_async_copy(closing, env_raw.at[core, chip], env_recv).start()

    @pl.when(b == 1)
    def _():
        pl.semaphore_signal(twin_ready, inc=1, device_id=twin, device_id_type=MESH)

    for q in range(7):
        @pl.when(q < rank)
        def _(q=q):
            pl.semaphore_signal(ready, inc=1, device_id=outer(q), device_id_type=MESH)

    def produce(n, carry):
        slot = n % 2
        regroup(n, slot)

        @pl.when(n < 6)
        def _():
            load(n + 2, slot).start()

        message(n, 0, 0, send_sem.at[0]).start()
        message(n, 1, 0, send_sem.at[1]).start()

        @pl.when(n == 4)
        def _():
            @pl.when(b == 0)
            def _():
                pl.semaphore_wait(twin_ready, 1)

            twin_rows.start()
            for t in range(4):
                half_copy(t).start()

        return carry

    lax.fori_loop(0, 7, produce, 0)
    regroup(7, 1)
    keep(0).start()
    message(7, 1, 0, near_send).start()

    def issue(h, final=False):
        j = h // 2
        dc = h % 2

        def start(n, carry):
            message(n, dc, j, send_sem.at[h], final).start()
            return carry

        lax.fori_loop(0, 7, start, 0)

        @pl.when(dc == 0)
        def _():
            keep(j, final).start()

        @pl.when(dc == 1)
        def _():
            message(7, 1, j, near_send, final).start()

    def drained(h):
        full_wait(recvbuf.at[0, 0, :, pl.ds(0, 7 * k_local), :], send_sem.at[h])

    k_all = own_half.shape[1]
    l_half = own_half.shape[2]

    def fill(half, where):
        def step(kb, carry):
            parity = kb // 4
            source = 4 * (kb % 4) + (core + parity) % 2
            row = pl.multiple_of(where * l_half, l_half)
            column = pl.multiple_of(parity * k_all + (kb % 4) * 128, 128)

            def turned(p):
                pieces = [
                    half[p, pl.ds(pl.multiple_of((source + extra) * k_local, k_local), k_local), :]
                    for extra in (0, 2)
                ]
                return jnp.concatenate(pieces, axis=0).T

            real = turned(0)
            imag = turned(1)
            matrix[pl.ds(row, l_half), pl.ds(column, 128)] = real
            matrix[pl.ds(row, l_half), pl.ds(k_all // 2 + column, 128)] = -imag
            matrix[pl.ds(2 * l_half + row, l_half), pl.ds(column, 128)] = imag
            matrix[pl.ds(2 * l_half + row, l_half), pl.ds(k_all // 2 + column, 128)] = real
            return carry

        lax.fori_loop(0, k_all // 128, step, 0)

    issue(2)
    full_wait(env_raw.at[core], env_recv)
    env_share.start()
    own_copy.wait()

    for h in range(4 - DEPTH):
        drained(h)
    issue(3)
    full_wait(env_raw.at[1 - core], share_recv)
    env[...] = env_raw[...].astype(F32)

    def gather_env(n, sums):
        g = group(n)

        def row(t, sums):
            cc = t // 8
            j = t % 8
            new = []
            for p in range(2):
                values = sendbuf[n, cc, j, p].astype(F32)
                for e in range(2):
                    weighted = values * env[cc, g, e, pl.ds(j, 1), :]
                    new.append(sums[2 * p + e] + (weighted[:, :128] + weighted[:, 128:]))
            return tuple(new)

        return lax.fori_loop(0, 16, row, sums)

    zero = jnp.zeros((k_local, 128), F32)
    sums = lax.fori_loop(0, 8, gather_env, (zero,) * 4)
    w = [jnp.sum(s, axis=1, keepdims=True) for s in sums]
    w_real = w[0] - w[3]
    w_imag = w[1] + w[2]

    k_mine = pl.ds(pl.multiple_of(me * k_local, k_local), k_local)
    blocks = l_half // 128
    full_wait(other_rows, rows_recv)
    for half, rows, where in ((own_half, k_mine, b), (other_rows, slice(None), 1 - b)):
        real = half[0, rows, :].astype(F32)
        imag = half[1, rows, :].astype(F32)
        closed_real = jnp.sum(real * w_real - imag * w_imag, axis=0, keepdims=True)
        closed_imag = jnp.sum(real * w_imag + imag * w_real, axis=0, keepdims=True)
        for t in range(blocks):
            part[where * blocks + t] = closed_real[:, t * 128:(t + 1) * 128]
            part[2 * blocks + where * blocks + t] = closed_imag[:, t * 128:(t + 1) * 128]

    def part_copy(step):
        to = (me + step) % 16
        return pltpu.make_async_remote_copy(
            src_ref=part.at[to], dst_ref=part_in.at[me], send_sem=part_send, recv_sem=part_recv,
            device_id=(c, to, b), device_id_type=MESH,
        )

    def mid_copy(q):
        return pltpu.make_async_remote_copy(
            src_ref=mid.at[0], dst_ref=mid_in.at[rank], send_sem=mid_send, recv_sem=mid_recv,
            device_id=outer(q), device_id_type=MESH,
        )

    def total_copy(step):
        return pltpu.make_async_remote_copy(
            src_ref=mid.at[1], dst_ref=total_in.at[me], send_sem=total_send, recv_sem=total_recv,
            device_id=peer(step), device_id_type=MESH,
        )

    for step in range(1, 16):
        part_copy(step).start()
    pltpu.make_async_copy(part.at[me], part_in.at[me], part_recv).start()

    drained(4 - DEPTH)
    issue(4)
    fill(own_half, b)

    drained(5 - DEPTH)
    issue(5)
    full_wait(part_in, part_recv)
    mid[0] = jnp.sum(part_in[...], axis=0)

    @pl.when(rank < 7)
    def _():
        pl.semaphore_wait(ready, 7 - rank)

    for q in range(8):
        @pl.when(q != rank)
        def _(q=q):
            mid_copy(q).start()

    pltpu.make_async_copy(mid.at[0], mid_in.at[rank], mid_recv).start()

    drained(6 - DEPTH)
    issue(6)
    full_wait(other_half.at[:, mine, :], half_recv)
    forward.start()
    full_wait(mid_in, mid_recv)
    mid[1] = jnp.sum(mid_in[...], axis=0)
    for step in range(1, 16):
        total_copy(step).start()
    pltpu.make_async_copy(mid.at[1], total_in.at[me], total_recv).start()

    drained(7 - DEPTH)
    issue(7)
    full_wait(other_half.at[:, theirs, :], fwd_recv)
    fill(other_half, 1 - b)

    drained(8 - DEPTH)
    issue(8)

    def choose():
        full_wait(total_in, total_recv)
        bits_copy.wait()
        chosen = bits_v[...]
        found = jnp.zeros((8, chosen.shape[1]), F32)
        for t in range(2 * blocks):
            rows = [total_in[t], total_in[2 * blocks + t], jnp.zeros((6, 128), F32)]
            spots = lax.broadcasted_iota(jnp.int32, (128, chosen.shape[1]), 0) + t * 128
            pick = jnp.where(spots == chosen, 1.0, 0.0).astype(F32)
            found = found + jnp.dot(
                jnp.concatenate(rows, axis=0), pick, precision=lax.Precision.HIGHEST, preferred_element_type=F32
            )
        amps_v[...] = found[:2]
        pltpu.make_async_copy(amps_v, amps, amp_sem).start()

    m_block = 512

    def chunk(j, carry):
        drained(j + 9 - DEPTH)

        @pl.when(j + 9 < 2 * ROUNDS - 2)
        def _():
            issue(j + 9)

        @pl.when(j + 9 >= 2 * ROUNDS - 2)
        def _():
            issue(j + 9, True)

        full_wait(recvbuf.at[j, 0], recv_sem.at[2 * j])
        full_wait(recvbuf.at[j, 1], recv_sem.at[2 * j + 1])

        def rows(m, carry):
            m0 = pl.multiple_of(m * m_block, m_block)
            right = recvbuf[j].reshape(2 * k_all, q_local)
            result = jnp.dot(matrix[pl.ds(m0, m_block), :], right, preferred_element_type=F32)
            for h in range(2):
                product[h, pl.ds(m0 * ROUNDS + j, m_block, stride=ROUNDS), :] = result[:, h * 128:(h + 1) * 128]
            return carry

        lax.fori_loop(0, matrix.shape[0] // m_block, rows, 0)

        @pl.when(j == 2)
        def _():
            choose()

        return carry

    lax.fori_loop(0, ROUNDS - 1, chunk, 0)

    def early_rows(m, carry):
        m0 = pl.multiple_of(m * m_block, m_block)
        right = latest[0].reshape(k_all, q_local)
        result = jnp.dot(matrix[pl.ds(m0, m_block), :k_all], right, preferred_element_type=F32)
        for h in range(2):
            spots = pl.ds(m0 * ROUNDS + ROUNDS - 1, m_block, stride=ROUNDS)
            product[h, spots, :] = result[:, h * 128:(h + 1) * 128]
        return carry

    full_wait(latest.at[0], recv_sem.at[2 * ROUNDS - 2])
    lax.fori_loop(0, matrix.shape[0] // m_block, early_rows, 0)
    full_wait(latest.at[1], recv_sem.at[2 * ROUNDS - 1])

    for h in range(2 * ROUNDS - DEPTH, 2 * ROUNDS):
        drained(h)
    full_wait(sendbuf.at[7, 0], near_send)
    full_wait(other_rows, rows_send)
    full_wait(env_raw.at[core], share_send)
    full_wait(other_half.at[:, mine, :], half_send)
    full_wait(other_half.at[:, mine, :], fwd_send)
    full_wait(env_raw.at[0, pl.ds(0, 7)], env_send)
    full_wait(part_in.at[pl.ds(0, 15)], part_send)
    full_wait(mid_in.at[pl.ds(0, 7)], mid_send)
    full_wait(total_in.at[pl.ds(0, 15)], total_send)
    full_wait(amps_v, amp_sem)


def write_kernel(product, latest, matrix, amps_in, out, amps, staging, spread, out_sem, amp_sem):
    amp_copy = pltpu.make_async_copy(amps_in, amps, amp_sem)
    amp_copy.start()
    blocks, rows = staging.shape[:2]
    per_part = out.shape[1] // rows
    half = matrix.shape[1] // 2
    last = ROUNDS - 1
    copies = []
    for t in range(blocks):
        right = latest[1].reshape(half, latest.shape[3])
        result = jnp.dot(matrix[t * rows:(t + 1) * rows, half:], right, preferred_element_type=F32)
        slot = t % 2
        for h in range(2):
            spread[slot, h, pl.ds(last, rows, stride=ROUNDS), :] = result[:, h * 128:(h + 1) * 128]
        for h in range(2):
            before = product[h, t * rows * ROUNDS:(t + 1) * rows * ROUNDS, :].reshape(rows, ROUNDS, 128)
            newest = spread[slot, h].reshape(rows, ROUNDS, 128)
            spot = lax.broadcasted_iota(jnp.int32, (rows, ROUNDS, 128), 1)
            whole = before + jnp.where(spot == last, newest, 0.0)
            staging[t, :, :, h * 128:(h + 1) * 128] = whole.astype(BF16)
        copy = pltpu.make_async_copy(
            staging.at[t], out.at[t // per_part, (t % per_part) * rows:(t % per_part + 1) * rows], out_sem.at[t]
        )
        copy.start()
        copies.append(copy)
    for copy in copies:
        copy.wait()
    amp_copy.wait()


def shards(stem_mantissa, exponents, branch, closing, bitstrings):
    stem = stem_mantissa[0]
    k_local, r_all, q_local = stem.shape[1:]
    k_all, l_half = branch.shape[1:]
    l_all = 2 * l_half
    r_local = closing.shape[1]
    expo = jnp.transpose(exponents[0], (0, 2, 1))
    bits = bitstrings.reshape(1, -1)
    dma = pltpu.SemaphoreType.DMA
    hbm = pl.BlockSpec(memory_space=pl.ANY)
    vmem = pl.BlockSpec(memory_space=pltpu.VMEM)
    product, received, matrix, amps = pl.pallas_call(
        contract_kernel,
        out_shape=(
            pltpu.VMEM((2, 2 * l_all * r_local, 128), F32),
            pltpu.VMEM((2, 2, k_all // 2, q_local), BF16),
            pltpu.VMEM((2 * l_all, 2 * k_all), BF16),
            jax.ShapeDtypeStruct((2, bits.shape[1]), F32),
        ),
        in_specs=[hbm] * 5,
        out_specs=(vmem, vmem, vmem, hbm),
        scratch_shapes=[
            pltpu.VMEM((2, 2, k_local, 16, q_local), BF16),
            pltpu.VMEM(expo.shape, jnp.int32),
            pltpu.VMEM((2, k_local, r_all), F32),
            pltpu.VMEM((2, 2, 256, 128), F32),
            pltpu.VMEM((8, 2, r_local, 2, k_local, q_local), BF16),
            pltpu.VMEM((r_local - 1, 2, 2, k_all // 2, q_local), BF16),
            pltpu.VMEM((2, k_all, l_half), BF16),
            pltpu.VMEM((2, k_all, l_half), BF16),
            pltpu.VMEM((2, k_local, l_half), BF16),
            pltpu.VMEM((2, 8) + closing.shape, BF16),
            pltpu.VMEM((2, 8) + closing.shape, F32),
            pltpu.VMEM(bits.shape, jnp.int32),
            pltpu.VMEM((16, 1, 128), F32),
            pltpu.VMEM((16, 1, 128), F32),
            pltpu.VMEM((2, 1, 128), F32),
            pltpu.VMEM((8, 1, 128), F32),
            pltpu.VMEM((16, 1, 128), F32),
            pltpu.VMEM((2, bits.shape[1]), F32),
            dma((2,)), dma((2,)), dma,
            dma((2 * ROUNDS,)), dma((2 * ROUNDS,)),
            dma, dma, dma, dma, dma, dma, dma, dma, dma, dma, dma, dma, dma, dma, dma, dma, dma, dma,
            pltpu.SemaphoreType.REGULAR, pltpu.SemaphoreType.REGULAR,
        ],
        compiler_params=pltpu.CompilerParams(
            collective_id=0, has_side_effects=True, vmem_limit_bytes=30 * 2**20
        ),
        cost_estimate=pl.CostEstimate(
            flops=2 * (2 * k_all) * (2 * l_all) * r_local * q_local, bytes_accessed=2 * stem.size, transcendentals=0
        ),
        name="exchange_and_contract",
    )(stem, expo, branch, closing, bits)

    rows = 256
    keep_vmem = [pltpu.with_memory_space_constraint(a, pltpu.VMEM) for a in (product, received, matrix)]
    new_block, amps = pl.pallas_call(
        write_kernel,
        out_shape=(
            jax.ShapeDtypeStruct((2, l_all, r_local, q_local), BF16),
            jax.ShapeDtypeStruct(amps.shape, F32),
        ),
        in_specs=[vmem, vmem, vmem, hbm],
        out_specs=(hbm, hbm),
        scratch_shapes=[
            pltpu.VMEM((2 * l_all // rows, rows, r_local, q_local), BF16),
            pltpu.VMEM((2, 2, rows * r_local, 128), F32),
            dma((2 * l_all // rows,)),
            dma,
        ],
        compiler_params=pltpu.CompilerParams(vmem_limit_bytes=30 * 2**20),
        name="finish_and_write",
    )(*keep_vmem, amps)
    return (new_block[None], amps)


def solution(mesh):
    return jax.shard_map(
        shards,
        mesh=mesh,
        in_specs=(
            P("cuts", None, "idx", None, "br"),
            P("cuts", "idx", None, "br"),
            P(None, None, "br"),
            P(None, "idx", "br"),
            P(),
        ),
        out_specs=(P("cuts", None, None, "idx", "br"), P()),
        check_vma=False,
    )
```

time: 114 us -> 107 us (0.939)
  Pallas kernels: 113 us -> 106 us
    pallas_call x1, Pallas kernels: 109 us -> 101 us  [shards(): pl.pallas_call(contract_kernel, out_shape=(pltpu.VMEM((2, 2 * l_all * r_l...]
where the time goes in v2:
time: 107 us
  Pallas kernels  106 us (99%)
    pallas_call x1, Pallas kernels, shards(): pl.pallas_call(contract_kernel, out_shape=(pltpu.VMEM((2, 2 * l_all * r_l...  101 us
    pallas_call x1, Pallas kernels, shards(): pl.pallas_call(write_kernel, out_shape=(jax.ShapeDtypeStruct((2, l_all, r...  4.93 us

profile of v2, /device:TPU:1, one launch (start us, length us, event | category | flops | bytes accessed | tf_op | source)
XLA Modules:
  0.0 106.6 jit_solution(511450330649195570)
XLA Ops:
  0.6 101.1 %exchange_and_contract.1 = (f32[2,16384,128]{2,1,0:T(8,128)S(1)}, bf16[2,2,512,256]{3,2,1,0:T(8,128)(2,1)S(1)}, bf16[2048,2048]{1,0:T(8,128)(2,1)S(1)}, f32[2,1024]{1,0:T(2,128)}) custom-call(bf16[2,64,128,256]{3,2,1,0:T(8,128)(2,1)} %bitcast.6, s32[64,2,128]{2,1,0:T(2,128)} %bitcast.8, bf16[2,1024,512]{2,1,0:T(8,128)(2,1)} %branch.1, ...), custom_call_target="tpu_custom_call" | custom-call | flops 17179869184 | bytes 8388608 | tf_op jit(solution)/shard_map/exchange_and_contract/pallas_call | solution.py:476
  101.7 4.9 %finish_and_write.1 = (bf16[2,1024,8,256]{3,2,1,0:T(8,128)(2,1)}, f32[2,1024]{1,0:T(2,128)}) custom-call(f32[2,16384,128]{2,1,0:T(8,128)S(1)} %get-tuple-element.8.product, bf16[2,2,512,256]{3,2,1,0:T(8,128)(2,1)S(1)} %get-tuple-element.9.latest, bf16[2048,2048]{1,0:T(8,128)(2,1)S(1)} %get-tuple-element.10.matrix, f32[2,1024]{1,0:T(2,128)} %get-tuple-element.11.amps_in), custom_call_target="tpu_custom_call" | custom-call | tf_op jit(solution)/shard_map/finish_and_write/pallas_call | solution.py:521

commit v3 on v2

--- a/solution.py
+++ b/solution.py
@@ -10,6 +10,7 @@
 BF16 = jnp.bfloat16
 ROUNDS = 8
 DEPTH = 2
+SLOTS = 4
 
 
 def full_wait(ref, sem):
@@ -18,8 +19,8 @@
 
 def contract_kernel(
     stem, expo, branch, closing, bits,
-    product, latest, matrix, amps,
-    inbuf, raw_exp, scale, tiles, sendbuf, recvbuf, own_half, other_half, other_rows,
+    done, product, latest, matrix, amps,
+    inbuf, raw_exp, scale, tiles, sendbuf, recvbuf, first, own_half, other_half, other_rows,
     env_raw, env, bits_v, part, part_in, mid, mid_in, total_in, amps_v,
     in_sem, small_sem, half_sem, send_sem, recv_sem, near_send, half_send, half_recv, fwd_send, fwd_recv,
     rows_send, rows_recv, env_send, env_recv, share_send, share_recv, part_send, part_recv, mid_send, mid_recv, total_send, total_recv, amp_sem,
@@ -38,6 +39,11 @@
         dx = (2 + n % 2) * (1 - n // 4) + (1 - n % 2) * (n // 4)
         return ((z + dz) % 2) * 4 + (x + dx) % 4
 
+    def source_group(n):
+        dz = 1 - (n // 2) % 2
+        dx = (2 + n % 2) * (1 - n // 4) + (1 - n % 2) * (n // 4)
+        return ((z + dz) % 2) * 4 + (x + 4 - dx) % 4
+
     def peer(step):
         return (c, (me + step) % 16, b)
 
@@ -49,15 +55,16 @@
     twin = (c, (me + 8) % 16, 1 - b)
     sibling = (c, me + 1 - 2 * core, b)
 
-    def load(n, slot):
-        return pltpu.make_async_copy(
-            stem.at[:, :, pl.ds(pl.multiple_of(group(n) * 16, 16), 16), :], inbuf.at[slot], in_sem.at[slot]
-        )
+    def load(step):
+        rows = pl.ds(pl.multiple_of(group(step % 8) * 16, 16), 16)
+        columns = pl.ds(pl.multiple_of((step // 8) * 128, 128), 128)
+        slot = step % SLOTS
+        return pltpu.make_async_copy(stem.at[:, :, rows, columns], inbuf.at[slot], in_sem.at[slot])
 
     exp_copy = pltpu.make_async_copy(expo, raw_exp, small_sem.at[0])
     exp_copy.start()
-    load(0, 0).start()
-    load(1, 1).start()
+    for step in range(SLOTS):
+        load(step).start()
 
     barrier = pltpu.get_barrier_semaphore()
     for step in range(1, 16):
@@ -85,46 +92,49 @@
         high = (1 + 15 * ((shifted // 4) % 2)).astype(F32)
         scale[h] = 0.25 * low * middle * high
 
-    def landing(dc, j, final):
-        rows = pl.ds(pl.multiple_of((me // 2) * k_local, k_local), k_local)
-        return latest.at[dc, :, rows, :] if final else recvbuf.at[j, dc, :, rows, :]
+    def landing(n, dc, j, final):
+        rows = pl.ds(pl.multiple_of((n % 4) * k_local, k_local), k_local)
+        quarter = 2 * dc + n // 4
+        return latest.at[quarter, :, rows, :] if final else recvbuf.at[j, quarter, :, rows, :]
 
     def message(n, dc, j, sem, final=False):
         cc = (core + dc) % 2
         return pltpu.make_async_remote_copy(
             src_ref=sendbuf.at[n, cc, j],
-            dst_ref=landing(dc, j, final),
+            dst_ref=landing(n, dc, j, final),
             send_sem=sem,
-            recv_sem=recv_sem.at[2 * j + dc],
+            recv_sem=recv_sem.at[4 * j + 2 * dc + n // 4],
             device_id=(c, group(n) * 2 + cc, b),
             device_id_type=MESH,
         )
 
     def keep(j, final=False):
-        return pltpu.make_async_copy(sendbuf.at[7, core, j], landing(0, j, final), recv_sem.at[2 * j])
-
-    def regroup(n, slot):
-        g = group(n)
-        turn = (128 - g * 16) % 128
-        load(n, slot).wait()
-
-        def step(kb, carry):
+        return pltpu.make_async_copy(sendbuf.at[7, core, j], landing(7, 0, j, final), recv_sem.at[4 * j + 1])
+
+    def regroup(step):
+        n = step % 8
+        h = step // 8
+        slot = step % SLOTS
+        turn = (128 - group(n) * 16) % 128
+        load(step).wait()
+
+        def part_of_k(kb, carry):
             k0 = pl.multiple_of(kb * 16, 16)
-            factors = [pltpu.roll(scale[h, pl.ds(k0, 16), :], turn, 1) for h in range(2)]
+            factors = pltpu.roll(scale[h, pl.ds(k0, 16), :], turn, 1)
             for p in range(2):
-                for h in range(2):
-                    block = inbuf[slot, p, pl.ds(k0, 16), :, h * 128:(h + 1) * 128]
-                    tiles[p, h] = block.astype(F32).reshape(256, 128)
-            for h in range(2):
-                for r in range(16):
-                    factor = jnp.broadcast_to(factors[h][:, r:r + 1], (16, 128))
-                    for p in range(2):
-                        rows = tiles[p, h, pl.ds(r, 16, stride=16), :] * factor
-                        sendbuf[n, r // 8, r % 8, p, pl.ds(k0, 16), h * 128:(h + 1) * 128] = rows.astype(BF16)
+                tiles[p] = inbuf[slot, p, pl.ds(k0, 16)].astype(F32).reshape(256, 128)
+            for r in range(16):
+                factor = jnp.broadcast_to(factors[:, r:r + 1], (16, 128))
+                spot = (r % 2) * 128
+                for p in range(2):
+                    rows = tiles[p, pl.ds(r, 16, stride=16), :] * factor
+                    sendbuf[n, r // 8, 4 * h + r % 8 // 2, p, pl.ds(k0, 16), spot:spot + 128] = rows.astype(BF16)
             return carry
 
-        lax.fori_loop(0, k_local // 16, step, 0)
-
+        lax.fori_loop(0, k_local // 16, part_of_k, 0)
+
+    regroup(0)
+    load(SLOTS).start()
     pl.semaphore_wait(barrier, 15 + rank + b)
 
     chip = me // 2
@@ -161,9 +171,6 @@
         dst_ref=other_rows, send_sem=rows_send, recv_sem=rows_recv, device_id=twin, device_id_type=MESH,
     )
 
-    for step in range(1, 8):
-        env_copy(step).start()
-    pltpu.make_async_copy(closing, env_raw.at[core, chip], env_recv).start()
 
     @pl.when(b == 1)
     def _():
@@ -174,14 +181,15 @@
         def _(q=q):
             pl.semaphore_signal(ready, inc=1, device_id=outer(q), device_id_type=MESH)
 
+    message(0, 0, 0, send_sem.at[0]).start()
+    message(0, 1, 0, send_sem.at[1]).start()
+    for step in range(1, 8):
+        env_copy(step).start()
+    pltpu.make_async_copy(closing, env_raw.at[core, chip], env_recv).start()
+
     def produce(n, carry):
-        slot = n % 2
-        regroup(n, slot)
-
-        @pl.when(n < 6)
-        def _():
-            load(n + 2, slot).start()
-
+        regroup(n)
+        load(n + SLOTS).start()
         message(n, 0, 0, send_sem.at[0]).start()
         message(n, 1, 0, send_sem.at[1]).start()
 
@@ -197,8 +205,9 @@
 
         return carry
 
-    lax.fori_loop(0, 7, produce, 0)
-    regroup(7, 1)
+    lax.fori_loop(1, 7, produce, 0)
+    regroup(7)
+    load(7 + SLOTS).start()
     keep(0).start()
     message(7, 1, 0, near_send).start()
 
@@ -221,36 +230,47 @@
             message(7, 1, j, near_send, final).start()
 
     def drained(h):
-        full_wait(recvbuf.at[0, 0, :, pl.ds(0, 7 * k_local), :], send_sem.at[h])
+        full_wait(sendbuf.at[0, 0, pl.ds(0, 7)], send_sem.at[h])
 
     k_all = own_half.shape[1]
     l_half = own_half.shape[2]
 
     def fill(half, where):
         def step(kb, carry):
-            parity = kb // 4
-            source = 4 * (kb % 4) + (core + parity) % 2
+            quarter = kb // 2
+            place = (quarter % 2) * 4 + (kb % 2) * 2
             row = pl.multiple_of(where * l_half, l_half)
-            column = pl.multiple_of(parity * k_all + (kb % 4) * 128, 128)
+            column = pl.multiple_of(quarter * (k_all // 2) + (kb % 2) * 128, 128)
 
             def turned(p):
-                pieces = [
-                    half[p, pl.ds(pl.multiple_of((source + extra) * k_local, k_local), k_local), :]
-                    for extra in (0, 2)
-                ]
+                pieces = []
+                for extra in (0, 1):
+                    source = 2 * source_group(place + extra) + (core + quarter // 2) % 2
+                    pieces.append(half[p, pl.ds(pl.multiple_of(source * k_local, k_local), k_local), :])
                 return jnp.concatenate(pieces, axis=0).T
 
             real = turned(0)
             imag = turned(1)
             matrix[pl.ds(row, l_half), pl.ds(column, 128)] = real
-            matrix[pl.ds(row, l_half), pl.ds(k_all // 2 + column, 128)] = -imag
+            matrix[pl.ds(row, l_half), pl.ds(k_all // 4 + column, 128)] = -imag
             matrix[pl.ds(2 * l_half + row, l_half), pl.ds(column, 128)] = imag
-            matrix[pl.ds(2 * l_half + row, l_half), pl.ds(k_all // 2 + column, 128)] = real
+            matrix[pl.ds(2 * l_half + row, l_half), pl.ds(k_all // 4 + column, 128)] = real
             return carry
 
         lax.fori_loop(0, k_all // 128, step, 0)
 
     issue(2)
+
+    def second_half(step, carry):
+        regroup(step)
+
+        @pl.when(step + SLOTS < 16)
+        def _():
+            load(step + SLOTS).start()
+
+        return carry
+
+    lax.fori_loop(8, 16, second_half, 0)
     full_wait(env_raw.at[core], env_recv)
     env_share.start()
     own_copy.wait()
@@ -259,23 +279,26 @@
         drained(h)
     issue(3)
     full_wait(env_raw.at[1 - core], share_recv)
-    env[...] = env_raw[...].astype(F32)
+    for h in range(2):
+        env[:, :, :, h] = env_raw[:, :, :, :, h * 128:(h + 1) * 128].astype(F32)
 
     def gather_env(n, sums):
         g = group(n)
 
         def row(t, sums):
-            cc = t // 8
-            j = t % 8
-            new = []
-            for p in range(2):
-                values = sendbuf[n, cc, j, p].astype(F32)
-                for e in range(2):
-                    weighted = values * env[cc, g, e, pl.ds(j, 1), :]
-                    new.append(sums[2 * p + e] + (weighted[:, :128] + weighted[:, 128:]))
+            cc = t // 4
+            pair = t % 4
+            new = list(sums)
+            for h in range(2):
+                for p in range(2):
+                    values = sendbuf[n, cc, 4 * h + pair, p].astype(F32)
+                    for e in range(2):
+                        for s in range(2):
+                            weight = env[cc, g, e, h, pl.ds(2 * pair + s, 1), :]
+                            new[2 * p + e] = new[2 * p + e] + values[:, s * 128:(s + 1) * 128] * weight
             return tuple(new)
 
-        return lax.fori_loop(0, 16, row, sums)
+        return lax.fori_loop(0, 8, row, sums)
 
     zero = jnp.zeros((k_local, 128), F32)
     sums = lax.fori_loop(0, 8, gather_env, (zero,) * 4)
@@ -373,50 +396,74 @@
 
     m_block = 512
 
-    def chunk(j, carry):
-        drained(j + 9 - DEPTH)
-
-        @pl.when(j + 9 < 2 * ROUNDS - 2)
-        def _():
-            issue(j + 9)
-
-        @pl.when(j + 9 >= 2 * ROUNDS - 2)
-        def _():
-            issue(j + 9, True)
-
-        full_wait(recvbuf.at[j, 0], recv_sem.at[2 * j])
-        full_wait(recvbuf.at[j, 1], recv_sem.at[2 * j + 1])
+    def tile_rows(m0, j, s):
+        return pl.ds(m0 * ROUNDS + 2 * (j % 4) + s, m_block, stride=ROUNDS)
+
+    def chunk(target):
+        def run(j, carry):
+            drained(j + 9 - DEPTH)
+
+            @pl.when(j + 9 < 2 * ROUNDS - 2)
+            def _():
+                issue(j + 9)
+
+            @pl.when(j + 9 >= 2 * ROUNDS - 2)
+            def _():
+                issue(j + 9, True)
+
+            for quarter in range(4):
+                full_wait(recvbuf.at[j, quarter], recv_sem.at[4 * j + quarter])
+
+            def rows(m, carry):
+                m0 = pl.multiple_of(m * m_block, m_block)
+                right = recvbuf[j].reshape(2 * k_all, q_local)
+                result = jnp.dot(matrix[pl.ds(m0, m_block), :], right, preferred_element_type=F32)
+                for s in range(2):
+                    target[tile_rows(m0, j, s), :] = result[:, s * 128:(s + 1) * 128]
+                return carry
+
+            lax.fori_loop(0, matrix.shape[0] // m_block, rows, 0)
+
+            @pl.when(j == 2)
+            def _():
+                choose()
+
+            return carry
+
+        return run
+
+    lax.fori_loop(0, ROUNDS // 2, chunk(first), 0)
+
+    def settle(t, carry):
+        t0 = pl.multiple_of(t * 128, 128)
+        block = first[pl.ds(pl.multiple_of(t0 * ROUNDS, 128 * ROUNDS), 128 * ROUNDS), :]
+        done[pl.ds(t0, 128)] = block.reshape(128, ROUNDS, 128).astype(BF16)
+        return carry
+
+    lax.fori_loop(0, matrix.shape[0] // 128, settle, 0)
+    lax.fori_loop(ROUNDS // 2, ROUNDS - 1, chunk(product), 0)
+
+    def early(low, high):
+        columns = slice(low * (k_all // 2), high * (k_all // 2))
 
         def rows(m, carry):
             m0 = pl.multiple_of(m * m_block, m_block)
-            right = recvbuf[j].reshape(2 * k_all, q_local)
-            result = jnp.dot(matrix[pl.ds(m0, m_block), :], right, preferred_element_type=F32)
-            for h in range(2):
-                product[h, pl.ds(m0 * ROUNDS + j, m_block, stride=ROUNDS), :] = result[:, h * 128:(h + 1) * 128]
+            right = latest[low:high].reshape((high - low) * (k_all // 2), q_local)
+            result = jnp.dot(matrix[pl.ds(m0, m_block), columns], right, preferred_element_type=F32)
+            for s in range(2):
+                spots = tile_rows(m0, ROUNDS - 1, s)
+                piece = result[:, s * 128:(s + 1) * 128]
+                product[spots, :] = piece if low == 0 else product[spots, :] + piece
             return carry
 
         lax.fori_loop(0, matrix.shape[0] // m_block, rows, 0)
 
-        @pl.when(j == 2)
-        def _():
-            choose()
-
-        return carry
-
-    lax.fori_loop(0, ROUNDS - 1, chunk, 0)
-
-    def early_rows(m, carry):
-        m0 = pl.multiple_of(m * m_block, m_block)
-        right = latest[0].reshape(k_all, q_local)
-        result = jnp.dot(matrix[pl.ds(m0, m_block), :k_all], right, preferred_element_type=F32)
-        for h in range(2):
-            spots = pl.ds(m0 * ROUNDS + ROUNDS - 1, m_block, stride=ROUNDS)
-            product[h, spots, :] = result[:, h * 128:(h + 1) * 128]
-        return carry
-
-    full_wait(latest.at[0], recv_sem.at[2 * ROUNDS - 2])
-    lax.fori_loop(0, matrix.shape[0] // m_block, early_rows, 0)
-    full_wait(latest.at[1], recv_sem.at[2 * ROUNDS - 1])
+    last = 4 * (ROUNDS - 1)
+    full_wait(latest.at[0], recv_sem.at[last])
+    full_wait(latest.at[1], recv_sem.at[last + 1])
+    early(0, 2)
+    full_wait(latest.at[2], recv_sem.at[last + 2])
+    full_wait(latest.at[3], recv_sem.at[last + 3])
 
     for h in range(2 * ROUNDS - DEPTH, 2 * ROUNDS):
         drained(h)
@@ -432,33 +479,60 @@
     full_wait(amps_v, amp_sem)
 
 
-def write_kernel(product, latest, matrix, amps_in, out, amps, staging, spread, out_sem, amp_sem):
+def write_kernel(
+    done, product, latest, matrix, amps_in, out, amps, staging, spread, done_sem, out_sem, amp_sem
+):
     amp_copy = pltpu.make_async_copy(amps_in, amps, amp_sem)
     amp_copy.start()
     blocks, rows = staging.shape[:2]
-    per_part = out.shape[1] // rows
-    half = matrix.shape[1] // 2
-    last = ROUNDS - 1
-    copies = []
-    for t in range(blocks):
-        right = latest[1].reshape(half, latest.shape[3])
-        result = jnp.dot(matrix[t * rows:(t + 1) * rows, half:], right, preferred_element_type=F32)
-        slot = t % 2
-        for h in range(2):
-            spread[slot, h, pl.ds(last, rows, stride=ROUNDS), :] = result[:, h * 128:(h + 1) * 128]
-        for h in range(2):
-            before = product[h, t * rows * ROUNDS:(t + 1) * rows * ROUNDS, :].reshape(rows, ROUNDS, 128)
-            newest = spread[slot, h].reshape(rows, ROUNDS, 128)
+    l_all = out.shape[1]
+    per_part = l_all // rows
+    quarter = matrix.shape[1] // 4
+    big = spread.shape[0] // ROUNDS
+    whole = [
+        pltpu.make_async_copy(done.at[pl.ds(p * l_all, l_all)], out.at[p, :, :, pl.ds(0, 128)], done_sem.at[p])
+        for p in range(2)
+    ]
+    for copy in whole:
+        copy.start()
+
+    def copy(t):
+        return pltpu.make_async_copy(
+            staging.at[t],
+            out.at[t // per_part, pl.ds((t % per_part) * rows, rows), :, pl.ds(128, 128)],
+            out_sem.at[t],
+        )
+
+    def block(m, carry):
+        m0 = pl.multiple_of(m * big, big)
+        right = latest[2:].reshape(2 * quarter, latest.shape[3])
+        result = jnp.dot(matrix[pl.ds(m0, big), 2 * quarter:], right, preferred_element_type=F32)
+        for s in range(2):
+            spread[pl.ds(ROUNDS - 2 + s, big, stride=ROUNDS), :] = result[:, s * 128:(s + 1) * 128]
+
+        def piece(i, carry):
+            t = m * (big // rows) + i
+            spots = pl.ds(pl.multiple_of(t * rows * ROUNDS, rows * ROUNDS), rows * ROUNDS)
+            local = pl.ds(pl.multiple_of(i * rows * ROUNDS, rows * ROUNDS), rows * ROUNDS)
+            before = product[spots, :].reshape(rows, ROUNDS, 128)
+            newest = spread[local, :].reshape(rows, ROUNDS, 128)
             spot = lax.broadcasted_iota(jnp.int32, (rows, ROUNDS, 128), 1)
-            whole = before + jnp.where(spot == last, newest, 0.0)
-            staging[t, :, :, h * 128:(h + 1) * 128] = whole.astype(BF16)
-        copy = pltpu.make_async_copy(
-            staging.at[t], out.at[t // per_part, (t % per_part) * rows:(t % per_part + 1) * rows], out_sem.at[t]
-        )
-        copy.start()
-        copies.append(copy)
-    for copy in copies:
-        copy.wait()
+            staging[t] = (before + jnp.where(spot >= ROUNDS - 2, newest, 0.0)).astype(BF16)
+            copy(t).start()
+            return carry
+
+        lax.fori_loop(0, big // rows, piece, 0)
+        return carry
+
+    lax.fori_loop(0, matrix.shape[0] // big, block, 0)
+
+    def finish(t, carry):
+        copy(t).wait()
+        return carry
+
+    lax.fori_loop(0, blocks, finish, 0)
+    for copy_of_part in whole:
+        copy_of_part.wait()
     amp_copy.wait()
 
 
@@ -473,28 +547,30 @@
     dma = pltpu.SemaphoreType.DMA
     hbm = pl.BlockSpec(memory_space=pl.ANY)
     vmem = pl.BlockSpec(memory_space=pltpu.VMEM)
-    product, received, matrix, amps = pl.pallas_call(
+    done, product, received, matrix, amps = pl.pallas_call(
         contract_kernel,
         out_shape=(
-            pltpu.VMEM((2, 2 * l_all * r_local, 128), F32),
-            pltpu.VMEM((2, 2, k_all // 2, q_local), BF16),
+            pltpu.VMEM((2 * l_all, r_local, 128), BF16),
+            pltpu.VMEM((2 * l_all * r_local, 128), F32),
+            pltpu.VMEM((4, 2, k_all // 4, q_local), BF16),
             pltpu.VMEM((2 * l_all, 2 * k_all), BF16),
             jax.ShapeDtypeStruct((2, bits.shape[1]), F32),
         ),
         in_specs=[hbm] * 5,
-        out_specs=(vmem, vmem, vmem, hbm),
+        out_specs=(vmem, vmem, vmem, vmem, hbm),
         scratch_shapes=[
-            pltpu.VMEM((2, 2, k_local, 16, q_local), BF16),
+            pltpu.VMEM((SLOTS, 2, k_local, 16, 128), BF16),
             pltpu.VMEM(expo.shape, jnp.int32),
             pltpu.VMEM((2, k_local, r_all), F32),
-            pltpu.VMEM((2, 2, 256, 128), F32),
+            pltpu.VMEM((2, 256, 128), F32),
             pltpu.VMEM((8, 2, r_local, 2, k_local, q_local), BF16),
-            pltpu.VMEM((r_local - 1, 2, 2, k_all // 2, q_local), BF16),
+            pltpu.VMEM((r_local - 1, 4, 2, k_all // 4, q_local), BF16),
+            pltpu.VMEM((2 * l_all * r_local, 128), F32),
             pltpu.VMEM((2, k_all, l_half), BF16),
             pltpu.VMEM((2, k_all, l_half), BF16),
             pltpu.VMEM((2, k_local, l_half), BF16),
             pltpu.VMEM((2, 8) + closing.shape, BF16),
-            pltpu.VMEM((2, 8) + closing.shape, F32),
+            pltpu.VMEM((2, 8, 2, 2, r_local, 128), F32),
             pltpu.VMEM(bits.shape, jnp.int32),
             pltpu.VMEM((16, 1, 128), F32),
             pltpu.VMEM((16, 1, 128), F32),
@@ -502,13 +578,13 @@
             pltpu.VMEM((8, 1, 128), F32),
             pltpu.VMEM((16, 1, 128), F32),
             pltpu.VMEM((2, bits.shape[1]), F32),
-            dma((2,)), dma((2,)), dma,
-            dma((2 * ROUNDS,)), dma((2 * ROUNDS,)),
+            dma((SLOTS,)), dma((2,)), dma,
+            dma((2 * ROUNDS,)), dma((4 * ROUNDS,)),
             dma, dma, dma, dma, dma, dma, dma, dma, dma, dma, dma, dma, dma, dma, dma, dma, dma, dma,
             pltpu.SemaphoreType.REGULAR, pltpu.SemaphoreType.REGULAR,
         ],
         compiler_params=pltpu.CompilerParams(
-            collective_id=0, has_side_effects=True, vmem_limit_bytes=30 * 2**20
+            collective_id=0, has_side_effects=True, vmem_limit_bytes=34 * 2**20
         ),
         cost_estimate=pl.CostEstimate(
             flops=2 * (2 * k_all) * (2 * l_all) * r_local * q_local, bytes_accessed=2 * stem.size, transcendentals=0
@@ -516,23 +592,25 @@
         name="exchange_and_contract",
     )(stem, expo, branch, closing, bits)
 
-    rows = 256
-    keep_vmem = [pltpu.with_memory_space_constraint(a, pltpu.VMEM) for a in (product, received, matrix)]
+    rows = 128
+    big = 512
+    keep_vmem = [pltpu.with_memory_space_constraint(a, pltpu.VMEM) for a in (done, product, received, matrix)]
     new_block, amps = pl.pallas_call(
         write_kernel,
         out_shape=(
             jax.ShapeDtypeStruct((2, l_all, r_local, q_local), BF16),
             jax.ShapeDtypeStruct(amps.shape, F32),
         ),
-        in_specs=[vmem, vmem, vmem, hbm],
+        in_specs=[vmem, vmem, vmem, vmem, hbm],
         out_specs=(hbm, hbm),
         scratch_shapes=[
-            pltpu.VMEM((2 * l_all // rows, rows, r_local, q_local), BF16),
-            pltpu.VMEM((2, 2, rows * r_local, 128), F32),
+            pltpu.VMEM((2 * l_all // rows, rows, r_local, 128), BF16),
+            pltpu.VMEM((big * r_local, 128), F32),
+            dma((2,)),
             dma((2 * l_all // rows,)),
             dma,
         ],
-        compiler_params=pltpu.CompilerParams(vmem_limit_bytes=30 * 2**20),
+        compiler_params=pltpu.CompilerParams(vmem_limit_bytes=34 * 2**20),
         name="finish_and_write",
     )(*keep_vmem, amps)
     return (new_block[None], amps)

time: 107 us -> 105 us (0.981)
  Pallas kernels: 106 us -> 104 us
    pallas_call x1, Pallas kernels: 4.93 us -> 3.53 us  [shards(): pl.pallas_call(write_kernel, out_shape=(jax.ShapeDtypeStruct((2, l_all, r...]
where the time goes in v3:
time: 105 us
  Pallas kernels  104 us (99%)
    pallas_call x1, Pallas kernels, shards(): pl.pallas_call(contract_kernel, out_shape=(pltpu.VMEM((2 * l_all, r_local...  101 us
    pallas_call x1, Pallas kernels, shards(): pl.pallas_call(write_kernel, out_shape=(jax.ShapeDtypeStruct((2, l_all, r...  3.53 us

profile of v3, /device:TPU:1, one launch (start us, length us, event | category | flops | bytes accessed | tf_op | source)
XLA Modules:
  0.0 105.1 jit_solution(10961058265271945226)
XLA Ops:
  0.6 100.9 %exchange_and_contract.1 = (bf16[2048,8,128]{2,1,0:T(8,128)(2,1)S(1)}, f32[16384,128]{1,0:T(8,128)S(1)}, bf16[4,2,256,256]{3,2,1,0:T(8,128)(2,1)S(1)}, bf16[2048,2048]{1,0:T(8,128)(2,1)S(1)}, f32[2,1024]{1,0:T(2,128)}) custom-call(bf16[2,64,128,256]{3,2,1,0:T(8,128)(2,1)} %bitcast.6, s32[64,2,128]{2,1,0:T(2,128)} %bitcast.8, bf16[2,1024,512]{2,1,0:T(8,128)(2,1)} %branch.1, ...), custom_call_target="tpu_custom_call" | custom-call | flops 17179869184 | bytes 8388608 | tf_op jit(solution)/shard_map/exchange_and_contract/pallas_call | solution.py:550
  101.6 3.5 %finish_and_write.1 = (bf16[2,1024,8,256]{3,2,1,0:T(8,128)(2,1)}, f32[2,1024]{1,0:T(2,128)}) custom-call(bf16[2048,8,128]{2,1,0:T(8,128)(2,1)S(1)} %get-tuple-element.9.done, f32[16384,128]{1,0:T(8,128)S(1)} %get-tuple-element.10.product, bf16[4,2,256,256]{3,2,1,0:T(8,128)(2,1)S(1)} %get-tuple-element.11.latest, ...), custom_call_target="tpu_custom_call" | custom-call | tf_op jit(solution)/shard_map/finish_and_write/pallas_call | solution.py:598

commit v4 on v3

--- a/solution.py
+++ b/solution.py
@@ -34,14 +34,17 @@
     z = me // 8
     k_local, q_local = sendbuf.shape[4:]
 
+    def steps(n, sender):
+        dz = (1 - (n // 2) % 2) % 2
+        dx = (2 + n % 2) * (1 - n // 4) + (1 - n % 2) * (n // 4)
+        return dz, dx * (1 + 2 * sender) % 4
+
     def group(n):
-        dz = 1 - (n // 2) % 2
-        dx = (2 + n % 2) * (1 - n // 4) + (1 - n % 2) * (n // 4)
+        dz, dx = steps(n, core)
         return ((z + dz) % 2) * 4 + (x + dx) % 4
 
-    def source_group(n):
-        dz = 1 - (n // 2) % 2
-        dx = (2 + n % 2) * (1 - n // 4) + (1 - n % 2) * (n // 4)
+    def source_group(n, sender):
+        dz, dx = steps(n, sender)
         return ((z + dz) % 2) * 4 + (x + 4 - dx) % 4
 
     def peer(step):
@@ -193,16 +196,6 @@
         message(n, 0, 0, send_sem.at[0]).start()
         message(n, 1, 0, send_sem.at[1]).start()
 
-        @pl.when(n == 4)
-        def _():
-            @pl.when(b == 0)
-            def _():
-                pl.semaphore_wait(twin_ready, 1)
-
-            twin_rows.start()
-            for t in range(4):
-                half_copy(t).start()
-
         return carry
 
     lax.fori_loop(1, 7, produce, 0)
@@ -245,7 +238,8 @@
             def turned(p):
                 pieces = []
                 for extra in (0, 1):
-                    source = 2 * source_group(place + extra) + (core + quarter // 2) % 2
+                    sender = (core + quarter // 2) % 2
+                    source = 2 * source_group(place + extra, sender) + sender
                     pieces.append(half[p, pl.ds(pl.multiple_of(source * k_local, k_local), k_local), :])
                 return jnp.concatenate(pieces, axis=0).T
 
@@ -260,6 +254,14 @@
         lax.fori_loop(0, k_all // 128, step, 0)
 
     issue(2)
+
+    @pl.when(b == 0)
+    def _():
+        pl.semaphore_wait(twin_ready, 1)
+
+    twin_rows.start()
+    for t in range(4):
+        half_copy(t).start()
 
     def second_half(step, carry):
         regroup(step)

time: 105 us -> 105 us (level)
  no operation moved by 1% of the time
where the time goes in v4:
time: 105 us
  Pallas kernels  104 us (99%)
    pallas_call x1, Pallas kernels, shards(): pl.pallas_call(contract_kernel, out_shape=(pltpu.VMEM((2 * l_all, r_local...  101 us
    pallas_call x1, Pallas kernels, shards(): pl.pallas_call(write_kernel, out_shape=(jax.ShapeDtypeStruct((2, l_all, r...  3.54 us

profile of v4, /device:TPU:1, one launch (start us, length us, event | category | flops | bytes accessed | tf_op | source)
XLA Modules:
  0.0 104.8 jit_solution(1268588406763525269)
XLA Ops:
  0.6 100.7 %exchange_and_contract.1 = (bf16[2048,8,128]{2,1,0:T(8,128)(2,1)S(1)}, f32[16384,128]{1,0:T(8,128)S(1)}, bf16[4,2,256,256]{3,2,1,0:T(8,128)(2,1)S(1)}, bf16[2048,2048]{1,0:T(8,128)(2,1)S(1)}, f32[2,1024]{1,0:T(2,128)}) custom-call(bf16[2,64,128,256]{3,2,1,0:T(8,128)(2,1)} %bitcast.6, s32[64,2,128]{2,1,0:T(2,128)} %bitcast.8, bf16[2,1024,512]{2,1,0:T(8,128)(2,1)} %branch.1, ...), custom_call_target="tpu_custom_call" | custom-call | flops 17179869184 | bytes 8388608 | tf_op jit(solution)/shard_map/exchange_and_contract/pallas_call | solution.py:552
  101.3 3.5 %finish_and_write.1 = (bf16[2,1024,8,256]{3,2,1,0:T(8,128)(2,1)}, f32[2,1024]{1,0:T(2,128)}) custom-call(bf16[2048,8,128]{2,1,0:T(8,128)(2,1)S(1)} %get-tuple-element.9.done, f32[16384,128]{1,0:T(8,128)S(1)} %get-tuple-element.10.product, bf16[4,2,256,256]{3,2,1,0:T(8,128)(2,1)S(1)} %get-tuple-element.11.latest, ...), custom_call_target="tpu_custom_call" | custom-call | tf_op jit(solution)/shard_map/finish_and_write/pallas_call | solution.py:600

commit v5 on v4

--- a/solution.py
+++ b/solution.py
@@ -186,9 +186,6 @@
 
     message(0, 0, 0, send_sem.at[0]).start()
     message(0, 1, 0, send_sem.at[1]).start()
-    for step in range(1, 8):
-        env_copy(step).start()
-    pltpu.make_async_copy(closing, env_raw.at[core, chip], env_recv).start()
 
     def produce(n, carry):
         regroup(n)
@@ -203,6 +200,9 @@
     load(7 + SLOTS).start()
     keep(0).start()
     message(7, 1, 0, near_send).start()
+    for step in range(1, 8):
+        env_copy(step).start()
+    pltpu.make_async_copy(closing, env_raw.at[core, chip], env_recv).start()
 
     def issue(h, final=False):
         j = h // 2

time: 105 us -> 105 us (level)
  no operation moved by 1% of the time
where the time goes in v5:
time: 105 us; the launch traced here: 104 us
  Pallas kernels  104 us (99%)
    pallas_call x1, Pallas kernels, shards(): pl.pallas_call(contract_kernel, out_shape=(pltpu.VMEM((2 * l_all, r_local...  100 us
    pallas_call x1, Pallas kernels, shards(): pl.pallas_call(write_kernel, out_shape=(jax.ShapeDtypeStruct((2, l_all, r...  3.53 us

profile of v5, /device:TPU:1, one launch (start us, length us, event | category | flops | bytes accessed | tf_op | source)
XLA Modules:
  0.0 104.4 jit_solution(12976787045653162689)
XLA Ops:
  0.6 100.3 %exchange_and_contract.1 = (bf16[2048,8,128]{2,1,0:T(8,128)(2,1)S(1)}, f32[16384,128]{1,0:T(8,128)S(1)}, bf16[4,2,256,256]{3,2,1,0:T(8,128)(2,1)S(1)}, bf16[2048,2048]{1,0:T(8,128)(2,1)S(1)}, f32[2,1024]{1,0:T(2,128)}) custom-call(bf16[2,64,128,256]{3,2,1,0:T(8,128)(2,1)} %bitcast.6, s32[64,2,128]{2,1,0:T(2,128)} %bitcast.8, bf16[2,1024,512]{2,1,0:T(8,128)(2,1)} %branch.1, ...), custom_call_target="tpu_custom_call" | custom-call | flops 17179869184 | bytes 8388608 | tf_op jit(solution)/shard_map/exchange_and_contract/pallas_call | solution.py:552
  100.9 3.5 %finish_and_write.1 = (bf16[2,1024,8,256]{3,2,1,0:T(8,128)(2,1)}, f32[2,1024]{1,0:T(2,128)}) custom-call(bf16[2048,8,128]{2,1,0:T(8,128)(2,1)S(1)} %get-tuple-element.9.done, f32[16384,128]{1,0:T(8,128)S(1)} %get-tuple-element.10.product, bf16[4,2,256,256]{3,2,1,0:T(8,128)(2,1)S(1)} %get-tuple-element.11.latest, ...), custom_call_target="tpu_custom_call" | custom-call | tf_op jit(solution)/shard_map/finish_and_write/pallas_call | solution.py:600

commit v6 on v5

--- a/solution.py
+++ b/solution.py
@@ -82,10 +82,6 @@
         def _(q=q):
             pl.semaphore_signal(barrier, inc=1, device_id=outer(q), device_id_type=MESH)
 
-    bits_copy = pltpu.make_async_copy(bits, bits_v, small_sem.at[1])
-    bits_copy.start()
-    own_copy = pltpu.make_async_copy(branch, own_half, half_sem)
-    own_copy.start()
 
     exp_copy.wait()
     for h in range(2):
@@ -200,6 +196,10 @@
     load(7 + SLOTS).start()
     keep(0).start()
     message(7, 1, 0, near_send).start()
+    bits_copy = pltpu.make_async_copy(bits, bits_v, small_sem.at[1])
+    bits_copy.start()
+    own_copy = pltpu.make_async_copy(branch, own_half, half_sem)
+    own_copy.start()
     for step in range(1, 8):
         env_copy(step).start()
     pltpu.make_async_copy(closing, env_raw.at[core, chip], env_recv).start()

time: 105 us -> 105 us (level)
  no operation moved by 1% of the time
where the time goes in v6:
time: 105 us; the launch traced here: 104 us
  Pallas kernels  104 us (99%)
    pallas_call x1, Pallas kernels, shards(): pl.pallas_call(contract_kernel, out_shape=(pltpu.VMEM((2 * l_all, r_local...  100 us
    pallas_call x1, Pallas kernels, shards(): pl.pallas_call(write_kernel, out_shape=(jax.ShapeDtypeStruct((2, l_all, r...  3.53 us

profile of v6, /device:TPU:1, one launch (start us, length us, event | category | flops | bytes accessed | tf_op | source)
XLA Modules:
  0.0 104.4 jit_solution(6001058350055014284)
XLA Ops:
  0.6 100.3 %exchange_and_contract.1 = (bf16[2048,8,128]{2,1,0:T(8,128)(2,1)S(1)}, f32[16384,128]{1,0:T(8,128)S(1)}, bf16[4,2,256,256]{3,2,1,0:T(8,128)(2,1)S(1)}, bf16[2048,2048]{1,0:T(8,128)(2,1)S(1)}, f32[2,1024]{1,0:T(2,128)}) custom-call(bf16[2,64,128,256]{3,2,1,0:T(8,128)(2,1)} %bitcast.6, s32[64,2,128]{2,1,0:T(2,128)} %bitcast.8, bf16[2,1024,512]{2,1,0:T(8,128)(2,1)} %branch.1, ...), custom_call_target="tpu_custom_call" | custom-call | flops 17179869184 | bytes 8388608 | tf_op jit(solution)/shard_map/exchange_and_contract/pallas_call | solution.py:552
  100.9 3.5 %finish_and_write.1 = (bf16[2,1024,8,256]{3,2,1,0:T(8,128)(2,1)}, f32[2,1024]{1,0:T(2,128)}) custom-call(bf16[2048,8,128]{2,1,0:T(8,128)(2,1)S(1)} %get-tuple-element.9.done, f32[16384,128]{1,0:T(8,128)S(1)} %get-tuple-element.10.product, bf16[4,2,256,256]{3,2,1,0:T(8,128)(2,1)S(1)} %get-tuple-element.11.latest, ...), custom_call_target="tpu_custom_call" | custom-call | tf_op jit(solution)/shard_map/finish_and_write/pallas_call | solution.py:600
